TPU v7x, 256 devices: a whole 4x4x8 slice. The times are simulated.
256 devices in a mesh: ctx: 16 (over x, z_hi), head: 16 (over y, z_lo, core).
Axes of the slice: x: 4, y: 4, z: 8 (z_hi: 4, z_lo: 2; z = z_hi * 2 + z_lo), core: 2. Of those that a mesh axis runs over, the one named last changes fastest.
Arguments:
- queries: bfloat16 [16384, 4096], P(('ctx', 'head')), may hold values from -200 to 200
- keys: bfloat16 [16384, 512], P(('ctx', 'head')), may hold values from -6 to 6
- values: bfloat16 [16384, 512], P(('ctx', 'head')), may hold values from -6 to 6
Outputs:
- attended: bfloat16 [16384, 4096], P(('ctx', 'head'))
All inputs are finite; a program needn't handle non-finite values.
Results may differ from a plain program's by a relative error of at most 0.0065.
Values may be sent and summed in bfloat16 or wider, within the bound.
A program may use at most 64 MiB of HBM per device.

v0:
```python
import math

import jax
import jax.numpy as jnp
from jax import lax
from jax.sharding import PartitionSpec as P

QH = 32
KVH = 4
HD = 128


def attend_block(state, query_block, key_rows, value_rows, query_first, key_first):
    maxima, totals, summed = state
    scale = 1.0 / math.sqrt(HD)
    scores = (
        jnp.einsum("tsgd,ksd->sgtk", query_block, key_rows, preferred_element_type=jnp.float32)
        * scale
    )
    query_pos = query_first + jnp.arange(query_block.shape[0], dtype=jnp.int32)
    key_pos = key_first + jnp.arange(key_rows.shape[0], dtype=jnp.int32)
    allowed = query_pos[:, None] >= key_pos[None, :]
    scores = jnp.where(allowed, scores, -1e30)
    new_max = jnp.maximum(maxima, jnp.max(scores, axis=-1))
    factor = jnp.exp(maxima - new_max)
    weights = jnp.exp(scores - new_max[..., None])
    totals = totals * factor + jnp.sum(weights, axis=-1)
    product = jnp.einsum(
        "sgtk,ksd->sgtd",
        weights.astype(jnp.bfloat16),
        value_rows,
        preferred_element_type=jnp.float32,
    )
    summed = summed * factor[..., None] + product
    return (new_max, totals, summed)


def make_work(query_block, query_first, taken, key_first):

    def work(current):
        return attend_block(current, query_block, taken[0], taken[1], query_first, key_first)

    return work


def keep_state(current):
    return current


def make_folder(query_parts, step_size):

    def folder(states, piece, start):
        step_len = min(step_size, piece.shape[1])
        count = piece.shape[1] // step_len

        def one_step(index, inner):
            key_first = index * step_len
            taken = lax.dynamic_slice_in_dim(piece, index * step_len, step_len, 1)
            updated = []
            for (query_block, query_first), current in zip(query_parts, inner):
                last_row = query_first + query_block.shape[0] - 1
                work = make_work(query_block, query_first, taken, key_first)
                updated.append(lax.cond(key_first <= last_row, work, keep_state, current))
            return tuple(updated)

        return lax.fori_loop(0, count, one_step, states)

    return folder


def empty_state(slots, group, rows):
    return (
        jnp.full((slots, group, rows), -1e30, jnp.float32),
        jnp.zeros((slots, group, rows), jnp.float32),
        jnp.zeros((slots, group, rows, HD), jnp.float32),
    )


def finish(state, head_local):
    maxima, totals, summed = state
    result = summed / totals[..., None]
    rows = result.shape[2]
    return result.transpose(2, 0, 1, 3).reshape(rows, head_local, HD).astype(jnp.bfloat16)


def shards(queries, keys, values):
    head_count = lax.axis_size("head")
    tok_rows = queries.shape[0]
    repeat = max(1, head_count // KVH)
    query_local = queries.reshape(tok_rows, QH, HD)
    paired = jnp.stack([keys.reshape(tok_rows, KVH, HD), values.reshape(tok_rows, KVH, HD)], 0)
    query_span = lax.all_to_all(query_local, "head", split_axis=1, concat_axis=0, tiled=True)
    span_len = query_span.shape[0]
    head_local = query_span.shape[1]
    slots = KVH * repeat // head_count
    group = head_local // slots
    query_block = query_span.reshape(span_len, slots, group, HD)
    ctx_index = lax.axis_index("ctx")
    query_first = ctx_index * span_len
    spread = jnp.repeat(paired, repeat, axis=2)
    paired_span = lax.all_to_all(spread, "head", split_axis=2, concat_axis=1, tiled=True)
    query_parts = [(query_block, query_first)]
    start_states = (empty_state(slots, group, span_len),)
    folder = make_folder(query_parts, span_len)
    states = folder(
        start_states, lax.all_gather(paired_span, "ctx", axis=1, tiled=True), jnp.int32(0)
    )
    result = finish(states[0], head_local)
    returned = lax.all_to_all(result, "head", split_axis=0, concat_axis=1, tiled=True)
    return returned.reshape(tok_rows, QH * HD)


def solution(mesh):
    return jax.shard_map(
        shards,
        mesh=mesh,
        in_specs=(P(("ctx", "head"), None), P(("ctx", "head"), None), P(("ctx", "head"), None)),
        out_specs=P(("ctx", "head"), None),
        check_vma=False,
    )
```

profile of v0, /device:TPU:231, one launch (start us, length us, event | category | flops | bytes accessed | tf_op | source)
XLA Modules:
  0.0 311.2 jit_solution(18398171506691050488)
XLA Ops:
  8.6 15.8 %all_to_all.48 = bf16[2,64,16,128]{3,1,0,2:T(8,128)(2,1)S(1)} all-to-all(bf16[2,64,16,128]{3,1,0,2:T(8,128)(2,1)S(1)} %bitcast.79), channel_id=1, replica_groups=mesh['ctx'=16,'head'=16] {'head'}, dimensions={2} | all-to-all | bytes 1048576 | tf_op jit(solution)/shard_map/all_to_all | solution.py:101
  26.2 4.6 %all-to-all-start.1 = ((bf16[64,32,128]{2,0,1:T(8,128)(2,1)}), bf16[64,32,128]{2,0,1:T(8,128)(2,1)S(1)}, u32[]{:S(2)}, u32[]{:S(2)}) async-start(bf16[64,32,128]{2,0,1:T(8,128)(2,1)} %copy_bitcast_fusion), calls=%async_computation.1 | async-start | bytes 1048576 | tf_op jit(solution)/shard_map/all_to_all | solution.py:92
  30.8 9.9 %all-to-all-done.1 = bf16[64,32,128]{2,0,1:T(8,128)(2,1)S(1)} async-done(((bf16[64,32,128]{2,0,1:T(8,128)(2,1)}), bf16[64,32,128]{2,0,1:T(8,128)(2,1)S(1)}, u32[]{:S(2)}, u32[]{:S(2)}) %all-to-all-start.1) | async-done | bytes 524320 | tf_op jit(solution)/shard_map/all_to_all | solution.py:92
  40.7 98.2 %all-gather.2.cloned.1.call-done = bf16[2,16384,1,128]{3,1,0,2:T(8,128)(2,1)} async-done(((bf16[2,1024,1,128]{3,1,0,2:T(8,128)(2,1)}), bf16[2,16384,1,128]{3,1,0,2:T(8,128)(2,1)}) %all-gather.2.cloned.1.call-update) | async-done | bytes 8388624 | tf_op jit(solution)/shard_map/all_gather | solution.py:106
  139.0 147.1 %while.19 = (s32[]{:T(128)}, f32[1,2,1024]{2,1,0:T(2,128)S(1)}, f32[1,2,1024]{2,1,0:T(2,128)S(1)}, f32[1,2,1024,128]{3,2,1,0:T(8,128)S(1)}, s32[]{:T(128)}, /*in...) while((s32[]{:T(128)}, f32[1,2,1024]{2,1,0:T(2,128)S(1)}, ...), condition=%wide.region_5.6_spmd, body=%wide.region_0.5_spmd.sunk | while | flops 1098391552 | bytes 32653616 | solution.py:66
  139.0 9.2 %conditional.2 = ((f32[1,2,1024]{2,1,0:T(2,128)S(1)}, f32[1,2,1024]{2,1,0:T(2,128)S(1)}, f32[1,2,1024,128]{3,2,1,0:T(8,128)S(1)})) conditional(s32[]{:T(128)} %convert_element_type.38, (f32[1,2,1024]{2,1,0:T(2,128)S(1)}, f32[1,2,1024]{2,1,0:T(2,128)S(1)}, f32[1,2,1024,128]{3,2,1,0:T(8,128)S(1)}) %tuple.56, (s32[]{:T(128)}, s32[]{:T(128)}, ...), branch_computations={%region_1.0_spmd, %region_2.4_spmd} | conditional | flops 1098391552 | bytes 32653410 | solution.py:63
  148.2 9.2 %conditional.2 = ((f32[1,2,1024]{2,1,0:T(2,128)S(1)}, f32[1,2,1024]{2,1,0:T(2,128)S(1)}, f32[1,2,1024,128]{3,2,1,0:T(8,128)S(1)})) conditional(s32[]{:T(128)} %convert_element_type.38, (f32[1,2,1024]{2,1,0:T(2,128)S(1)}, f32[1,2,1024]{2,1,0:T(2,128)S(1)}, f32[1,2,1024,128]{3,2,1,0:T(8,128)S(1)}) %tuple.56, (s32[]{:T(128)}, s32[]{:T(128)}, ...), branch_computations={%region_1.0_spmd, %region_2.4_spmd} | conditional | flops 1098391552 | bytes 32653410 | solution.py:63
  151.7 3.6 %fusion.10 = f32[1,2,1024,128]{3,2,1,0:T(8,128)S(1)} fusion(f32[1024,1024,2]{1,0,2:T(8,128)S(1)} %get-tuple-element.311, f32[2,1024]{1,0:T(2,128)S(1)} %bitcast.77, pred[1024,1024]{0,1:T(8,128)(4,1)S(1)} %broadcast_compare_fusion, f32[1,2,1024,128]{3,2,1,0:T(8,128)S(1)} %get-tuple-element.259, f32[2,1024]{1,0:T(2,128)S(1)} %get-tuple-element.308, ...), kind=kOutput, calls=%fused_computation.10 | convolution fusion | flops 545783808 | bytes 11812872 | tf_op jit(solution)/shard_map/while/body/eval_jaxpr/cond/branch_1_fun/sgtk,ksd->sgtd/dot_general | solution.py:28
  157.4 9.2 %conditional.2 = ((f32[1,2,1024]{2,1,0:T(2,128)S(1)}, f32[1,2,1024]{2,1,0:T(2,128)S(1)}, f32[1,2,1024,128]{3,2,1,0:T(8,128)S(1)})) conditional(s32[]{:T(128)} %convert_element_type.38, (f32[1,2,1024]{2,1,0:T(2,128)S(1)}, f32[1,2,1024]{2,1,0:T(2,128)S(1)}, f32[1,2,1024,128]{3,2,1,0:T(8,128)S(1)}) %tuple.56, (s32[]{:T(128)}, s32[]{:T(128)}, ...), branch_computations={%region_1.0_spmd, %region_2.4_spmd} | conditional | flops 1098391552 | bytes 32653410 | solution.py:63
  160.9 3.6 %fusion.10 = f32[1,2,1024,128]{3,2,1,0:T(8,128)S(1)} fusion(f32[1024,1024,2]{1,0,2:T(8,128)S(1)} %get-tuple-element.311, f32[2,1024]{1,0:T(2,128)S(1)} %bitcast.77, pred[1024,1024]{0,1:T(8,128)(4,1)S(1)} %broadcast_compare_fusion, f32[1,2,1024,128]{3,2,1,0:T(8,128)S(1)} %get-tuple-element.259, f32[2,1024]{1,0:T(2,128)S(1)} %get-tuple-element.308, ...), kind=kOutput, calls=%fused_computation.10 | convolution fusion | flops 545783808 | bytes 11812872 | tf_op jit(solution)/shard_map/while/body/eval_jaxpr/cond/branch_1_fun/sgtk,ksd->sgtd/dot_general | solution.py:28
  166.6 9.2 %conditional.2 = ((f32[1,2,1024]{2,1,0:T(2,128)S(1)}, f32[1,2,1024]{2,1,0:T(2,128)S(1)}, f32[1,2,1024,128]{3,2,1,0:T(8,128)S(1)})) conditional(s32[]{:T(128)} %convert_element_type.38, (f32[1,2,1024]{2,1,0:T(2,128)S(1)}, f32[1,2,1024]{2,1,0:T(2,128)S(1)}, f32[1,2,1024,128]{3,2,1,0:T(8,128)S(1)}) %tuple.56, (s32[]{:T(128)}, s32[]{:T(128)}, ...), branch_computations={%region_1.0_spmd, %region_2.4_spmd} | conditional | flops 1098391552 | bytes 32653410 | solution.py:63
  170.1 3.6 %fusion.10 = f32[1,2,1024,128]{3,2,1,0:T(8,128)S(1)} fusion(f32[1024,1024,2]{1,0,2:T(8,128)S(1)} %get-tuple-element.311, f32[2,1024]{1,0:T(2,128)S(1)} %bitcast.77, pred[1024,1024]{0,1:T(8,128)(4,1)S(1)} %broadcast_compare_fusion, f32[1,2,1024,128]{3,2,1,0:T(8,128)S(1)} %get-tuple-element.259, f32[2,1024]{1,0:T(2,128)S(1)} %get-tuple-element.308, ...), kind=kOutput, calls=%fused_computation.10 | convolution fusion | flops 545783808 | bytes 11812872 | tf_op jit(solution)/shard_map/while/body/eval_jaxpr/cond/branch_1_fun/sgtk,ksd->sgtd/dot_general | solution.py:28
  175.8 9.2 %conditional.2 = ((f32[1,2,1024]{2,1,0:T(2,128)S(1)}, f32[1,2,1024]{2,1,0:T(2,128)S(1)}, f32[1,2,1024,128]{3,2,1,0:T(8,128)S(1)})) conditional(s32[]{:T(128)} %convert_element_type.38, (f32[1,2,1024]{2,1,0:T(2,128)S(1)}, f32[1,2,1024]{2,1,0:T(2,128)S(1)}, f32[1,2,1024,128]{3,2,1,0:T(8,128)S(1)}) %tuple.56, (s32[]{:T(128)}, s32[]{:T(128)}, ...), branch_computations={%region_1.0_spmd, %region_2.4_spmd} | conditional | flops 1098391552 | bytes 32653410 | solution.py:63
  179.3 3.6 %fusion.10 = f32[1,2,1024,128]{3,2,1,0:T(8,128)S(1)} fusion(f32[1024,1024,2]{1,0,2:T(8,128)S(1)} %get-tuple-element.311, f32[2,1024]{1,0:T(2,128)S(1)} %bitcast.77, pred[1024,1024]{0,1:T(8,128)(4,1)S(1)} %broadcast_compare_fusion, f32[1,2,1024,128]{3,2,1,0:T(8,128)S(1)} %get-tuple-element.259, f32[2,1024]{1,0:T(2,128)S(1)} %get-tuple-element.308, ...), kind=kOutput, calls=%fused_computation.10 | convolution fusion | flops 545783808 | bytes 11812872 | tf_op jit(solution)/shard_map/while/body/eval_jaxpr/cond/branch_1_fun/sgtk,ksd->sgtd/dot_general | solution.py:28
  185.0 9.2 %conditional.2 = ((f32[1,2,1024]{2,1,0:T(2,128)S(1)}, f32[1,2,1024]{2,1,0:T(2,128)S(1)}, f32[1,2,1024,128]{3,2,1,0:T(8,128)S(1)})) conditional(s32[]{:T(128)} %convert_element_type.38, (f32[1,2,1024]{2,1,0:T(2,128)S(1)}, f32[1,2,1024]{2,1,0:T(2,128)S(1)}, f32[1,2,1024,128]{3,2,1,0:T(8,128)S(1)}) %tuple.56, (s32[]{:T(128)}, s32[]{:T(128)}, ...), branch_computations={%region_1.0_spmd, %region_2.4_spmd} | conditional | flops 1098391552 | bytes 32653410 | solution.py:63
  188.5 3.6 %fusion.10 = f32[1,2,1024,128]{3,2,1,0:T(8,128)S(1)} fusion(f32[1024,1024,2]{1,0,2:T(8,128)S(1)} %get-tuple-element.311, f32[2,1024]{1,0:T(2,128)S(1)} %bitcast.77, pred[1024,1024]{0,1:T(8,128)(4,1)S(1)} %broadcast_compare_fusion, f32[1,2,1024,128]{3,2,1,0:T(8,128)S(1)} %get-tuple-element.259, f32[2,1024]{1,0:T(2,128)S(1)} %get-tuple-element.308, ...), kind=kOutput, calls=%fused_computation.10 | convolution fusion | flops 545783808 | bytes 11812872 | tf_op jit(solution)/shard_map/while/body/eval_jaxpr/cond/branch_1_fun/sgtk,ksd->sgtd/dot_general | solution.py:28
  194.2 9.2 %conditional.2 = ((f32[1,2,1024]{2,1,0:T(2,128)S(1)}, f32[1,2,1024]{2,1,0:T(2,128)S(1)}, f32[1,2,1024,128]{3,2,1,0:T(8,128)S(1)})) conditional(s32[]{:T(128)} %convert_element_type.38, (f32[1,2,1024]{2,1,0:T(2,128)S(1)}, f32[1,2,1024]{2,1,0:T(2,128)S(1)}, f32[1,2,1024,128]{3,2,1,0:T(8,128)S(1)}) %tuple.56, (s32[]{:T(128)}, s32[]{:T(128)}, ...), branch_computations={%region_1.0_spmd, %region_2.4_spmd} | conditional | flops 1098391552 | bytes 32653410 | solution.py:63
  197.7 3.6 %fusion.10 = f32[1,2,1024,128]{3,2,1,0:T(8,128)S(1)} fusion(f32[1024,1024,2]{1,0,2:T(8,128)S(1)} %get-tuple-element.311, f32[2,1024]{1,0:T(2,128)S(1)} %bitcast.77, pred[1024,1024]{0,1:T(8,128)(4,1)S(1)} %broadcast_compare_fusion, f32[1,2,1024,128]{3,2,1,0:T(8,128)S(1)} %get-tuple-element.259, f32[2,1024]{1,0:T(2,128)S(1)} %get-tuple-element.308, ...), kind=kOutput, calls=%fused_computation.10 | convolution fusion | flops 545783808 | bytes 11812872 | tf_op jit(solution)/shard_map/while/body/eval_jaxpr/cond/branch_1_fun/sgtk,ksd->sgtd/dot_general | solution.py:28
  203.4 9.2 %conditional.2 = ((f32[1,2,1024]{2,1,0:T(2,128)S(1)}, f32[1,2,1024]{2,1,0:T(2,128)S(1)}, f32[1,2,1024,128]{3,2,1,0:T(8,128)S(1)})) conditional(s32[]{:T(128)} %convert_element_type.38, (f32[1,2,1024]{2,1,0:T(2,128)S(1)}, f32[1,2,1024]{2,1,0:T(2,128)S(1)}, f32[1,2,1024,128]{3,2,1,0:T(8,128)S(1)}) %tuple.56, (s32[]{:T(128)}, s32[]{:T(128)}, ...), branch_computations={%region_1.0_spmd, %region_2.4_spmd} | conditional | flops 1098391552 | bytes 32653410 | solution.py:63
  206.9 3.6 %fusion.10 = f32[1,2,1024,128]{3,2,1,0:T(8,128)S(1)} fusion(f32[1024,1024,2]{1,0,2:T(8,128)S(1)} %get-tuple-element.311, f32[2,1024]{1,0:T(2,128)S(1)} %bitcast.77, pred[1024,1024]{0,1:T(8,128)(4,1)S(1)} %broadcast_compare_fusion, f32[1,2,1024,128]{3,2,1,0:T(8,128)S(1)} %get-tuple-element.259, f32[2,1024]{1,0:T(2,128)S(1)} %get-tuple-element.308, ...), kind=kOutput, calls=%fused_computation.10 | convolution fusion | flops 545783808 | bytes 11812872 | tf_op jit(solution)/shard_map/while/body/eval_jaxpr/cond/branch_1_fun/sgtk,ksd->sgtd/dot_general | solution.py:28
  212.6 9.2 %conditional.2 = ((f32[1,2,1024]{2,1,0:T(2,128)S(1)}, f32[1,2,1024]{2,1,0:T(2,128)S(1)}, f32[1,2,1024,128]{3,2,1,0:T(8,128)S(1)})) conditional(s32[]{:T(128)} %convert_element_type.38, (f32[1,2,1024]{2,1,0:T(2,128)S(1)}, f32[1,2,1024]{2,1,0:T(2,128)S(1)}, f32[1,2,1024,128]{3,2,1,0:T(8,128)S(1)}) %tuple.56, (s32[]{:T(128)}, s32[]{:T(128)}, ...), branch_computations={%region_1.0_spmd, %region_2.4_spmd} | conditional | flops 1098391552 | bytes 32653410 | solution.py:63
  221.8 9.2 %conditional.2 = ((f32[1,2,1024]{2,1,0:T(2,128)S(1)}, f32[1,2,1024]{2,1,0:T(2,128)S(1)}, f32[1,2,1024,128]{3,2,1,0:T(8,128)S(1)})) conditional(s32[]{:T(128)} %convert_element_type.38, (f32[1,2,1024]{2,1,0:T(2,128)S(1)}, f32[1,2,1024]{2,1,0:T(2,128)S(1)}, f32[1,2,1024,128]{3,2,1,0:T(8,128)S(1)}) %tuple.56, (s32[]{:T(128)}, s32[]{:T(128)}, ...), branch_computations={%region_1.0_spmd, %region_2.4_spmd} | conditional | flops 1098391552 | bytes 32653410 | solution.py:63
  225.3 3.6 %fusion.10 = f32[1,2,1024,128]{3,2,1,0:T(8,128)S(1)} fusion(f32[1024,1024,2]{1,0,2:T(8,128)S(1)} %get-tuple-element.311, f32[2,1024]{1,0:T(2,128)S(1)} %bitcast.77, pred[1024,1024]{0,1:T(8,128)(4,1)S(1)} %broadcast_compare_fusion, f32[1,2,1024,128]{3,2,1,0:T(8,128)S(1)} %get-tuple-element.259, f32[2,1024]{1,0:T(2,128)S(1)} %get-tuple-element.308, ...), kind=kOutput, calls=%fused_computation.10 | convolution fusion | flops 545783808 | bytes 11812872 | tf_op jit(solution)/shard_map/while/body/eval_jaxpr/cond/branch_1_fun/sgtk,ksd->sgtd/dot_general | solution.py:28
  231.0 9.2 %conditional.2 = ((f32[1,2,1024]{2,1,0:T(2,128)S(1)}, f32[1,2,1024]{2,1,0:T(2,128)S(1)}, f32[1,2,1024,128]{3,2,1,0:T(8,128)S(1)})) conditional(s32[]{:T(128)} %convert_element_type.38, (f32[1,2,1024]{2,1,0:T(2,128)S(1)}, f32[1,2,1024]{2,1,0:T(2,128)S(1)}, f32[1,2,1024,128]{3,2,1,0:T(8,128)S(1)}) %tuple.56, (s32[]{:T(128)}, s32[]{:T(128)}, ...), branch_computations={%region_1.0_spmd, %region_2.4_spmd} | conditional | flops 1098391552 | bytes 32653410 | solution.py:63
  240.2 9.2 %conditional.2 = ((f32[1,2,1024]{2,1,0:T(2,128)S(1)}, f32[1,2,1024]{2,1,0:T(2,128)S(1)}, f32[1,2,1024,128]{3,2,1,0:T(8,128)S(1)})) conditional(s32[]{:T(128)} %convert_element_type.38, (f32[1,2,1024]{2,1,0:T(2,128)S(1)}, f32[1,2,1024]{2,1,0:T(2,128)S(1)}, f32[1,2,1024,128]{3,2,1,0:T(8,128)S(1)}) %tuple.56, (s32[]{:T(128)}, s32[]{:T(128)}, ...), branch_computations={%region_1.0_spmd, %region_2.4_spmd} | conditional | flops 1098391552 | bytes 32653410 | solution.py:63
  243.7 3.6 %fusion.10 = f32[1,2,1024,128]{3,2,1,0:T(8,128)S(1)} fusion(f32[1024,1024,2]{1,0,2:T(8,128)S(1)} %get-tuple-element.311, f32[2,1024]{1,0:T(2,128)S(1)} %bitcast.77, pred[1024,1024]{0,1:T(8,128)(4,1)S(1)} %broadcast_compare_fusion, f32[1,2,1024,128]{3,2,1,0:T(8,128)S(1)} %get-tuple-element.259, f32[2,1024]{1,0:T(2,128)S(1)} %get-tuple-element.308, ...), kind=kOutput, calls=%fused_computation.10 | convolution fusion | flops 545783808 | bytes 11812872 | tf_op jit(solution)/shard_map/while/body/eval_jaxpr/cond/branch_1_fun/sgtk,ksd->sgtd/dot_general | solution.py:28
  249.4 9.2 %conditional.2 = ((f32[1,2,1024]{2,1,0:T(2,128)S(1)}, f32[1,2,1024]{2,1,0:T(2,128)S(1)}, f32[1,2,1024,128]{3,2,1,0:T(8,128)S(1)})) conditional(s32[]{:T(128)} %convert_element_type.38, (f32[1,2,1024]{2,1,0:T(2,128)S(1)}, f32[1,2,1024]{2,1,0:T(2,128)S(1)}, f32[1,2,1024,128]{3,2,1,0:T(8,128)S(1)}) %tuple.56, (s32[]{:T(128)}, s32[]{:T(128)}, ...), branch_computations={%region_1.0_spmd, %region_2.4_spmd} | conditional | flops 1098391552 | bytes 32653410 | solution.py:63
  258.6 9.2 %conditional.2 = ((f32[1,2,1024]{2,1,0:T(2,128)S(1)}, f32[1,2,1024]{2,1,0:T(2,128)S(1)}, f32[1,2,1024,128]{3,2,1,0:T(8,128)S(1)})) conditional(s32[]{:T(128)} %convert_element_type.38, (f32[1,2,1024]{2,1,0:T(2,128)S(1)}, f32[1,2,1024]{2,1,0:T(2,128)S(1)}, f32[1,2,1024,128]{3,2,1,0:T(8,128)S(1)}) %tuple.56, (s32[]{:T(128)}, s32[]{:T(128)}, ...), branch_computations={%region_1.0_spmd, %region_2.4_spmd} | conditional | flops 1098391552 | bytes 32653410 | solution.py:63
  262.1 3.6 %fusion.10 = f32[1,2,1024,128]{3,2,1,0:T(8,128)S(1)} fusion(f32[1024,1024,2]{1,0,2:T(8,128)S(1)} %get-tuple-element.311, f32[2,1024]{1,0:T(2,128)S(1)} %bitcast.77, pred[1024,1024]{0,1:T(8,128)(4,1)S(1)} %broadcast_compare_fusion, f32[1,2,1024,128]{3,2,1,0:T(8,128)S(1)} %get-tuple-element.259, f32[2,1024]{1,0:T(2,128)S(1)} %get-tuple-element.308, ...), kind=kOutput, calls=%fused_computation.10 | convolution fusion | flops 545783808 | bytes 11812872 | tf_op jit(solution)/shard_map/while/body/eval_jaxpr/cond/branch_1_fun/sgtk,ksd->sgtd/dot_general | solution.py:28
  267.8 9.2 %conditional.2 = ((f32[1,2,1024]{2,1,0:T(2,128)S(1)}, f32[1,2,1024]{2,1,0:T(2,128)S(1)}, f32[1,2,1024,128]{3,2,1,0:T(8,128)S(1)})) conditional(s32[]{:T(128)} %convert_element_type.38, (f32[1,2,1024]{2,1,0:T(2,128)S(1)}, f32[1,2,1024]{2,1,0:T(2,128)S(1)}, f32[1,2,1024,128]{3,2,1,0:T(8,128)S(1)}) %tuple.56, (s32[]{:T(128)}, s32[]{:T(128)}, ...), branch_computations={%region_1.0_spmd, %region_2.4_spmd} | conditional | flops 1098391552 | bytes 32653410 | solution.py:63
  277.0 9.2 %conditional.2 = ((f32[1,2,1024]{2,1,0:T(2,128)S(1)}, f32[1,2,1024]{2,1,0:T(2,128)S(1)}, f32[1,2,1024,128]{3,2,1,0:T(8,128)S(1)})) conditional(s32[]{:T(128)} %convert_element_type.38, (f32[1,2,1024]{2,1,0:T(2,128)S(1)}, f32[1,2,1024]{2,1,0:T(2,128)S(1)}, f32[1,2,1024,128]{3,2,1,0:T(8,128)S(1)}) %tuple.56, (s32[]{:T(128)}, s32[]{:T(128)}, ...), branch_computations={%region_1.0_spmd, %region_2.4_spmd} | conditional | flops 1098391552 | bytes 32653410 | solution.py:63
  287.1 15.8 %all_to_all.49 = bf16[1024,2,128]{2,1,0:T(2,128)(2,1)S(1)} all-to-all(bf16[1024,2,128]{2,1,0:T(2,128)(2,1)S(1)} %copy.37), channel_id=1, replica_groups=mesh['ctx'=16,'head'=16] {'head'}, dimensions={0} | all-to-all | bytes 1048576 | tf_op jit(solution)/shard_map/all_to_all | solution.py:109
  (137 shorter events, 115.6 us)
Async XLA Ops:
  6.5 18.6 %copy-start = (bf16[64,4096]{1,0:T(8,128)(2,1)S(1)}, bf16[64,4096]{1,0:T(8,128)(2,1)}, u32[]{:S(2)}) copy-start(bf16[64,4096]{1,0:T(8,128)(2,1)} %param.7) | copy-start | bytes 1572868
  6.5 132.4 %all-gather.2.cloned.1.call-start = ((), (), s32[]{:S(2)}) async-start(), calls=%async_computation.3 | async-start | bytes 8912896 | tf_op jit(solution)/shard_map/all_gather | solution.py:106
  26.2 14.5 %all-to-all-start.1 = ((bf16[64,32,128]{2,0,1:T(8,128)(2,1)}), bf16[64,32,128]{2,0,1:T(8,128)(2,1)S(1)}, u32[]{:S(2)}, u32[]{:S(2)}) async-start(bf16[64,32,128]{2,0,1:T(8,128)(2,1)} %copy_bitcast_fusion), calls=%async_computation.1 | async-start | bytes 1048576 | tf_op jit(solution)/shard_map/all_to_all | solution.py:92
Sparse Core Ops, SparseCore 0:
  25.3 113.5 all-gather.1
where the time goes:
time: 313 us; the launch traced here: 311 us
  waiting for transfers between devices  108 us (35%)
  matrix products  102 us (33%)
  other arithmetic  43.5 us (14%)
  blocking collectives  31.5 us (10%)
  between operations  13.5 us (4%)
  local copies, waits for them, and re-layouts  5.96 us (2%)
  starting transfers between devices  4.63 us (1%)
    all_gather x1, waiting for transfers between devices, shards(): lax.all_gather(paired_span, 'ctx', axis=1, tiled=True)  98.2 us
    dot_general x16, matrix products, attend_block(): jnp.einsum('sgtk,ksd->sgtd', weights.astype(jnp.bfloat16), value_rows, pr...  58.1 us
    dot_general x16, matrix products, attend_block(): jnp.einsum('tsgd,ksd->sgtk', query_block, key_rows, preferred_element_typ...  44.4 us
    reduce_sum x16, other arithmetic, attend_block(): totals = totals * factor + jnp.sum(weights, axis=-1)  32 us
    all_to_all x1, blocking collectives, shards(): lax.all_to_all(result, 'head', split_axis=0, concat_axis=1, tiled=True)  15.8 us
    all_to_all x1, blocking collectives, shards(): lax.all_to_all(spread, 'head', split_axis=2, concat_axis=1, tiled=True)  15.8 us
    ge x16, other arithmetic, attend_block(): allowed = query_pos[:, None] >= key_pos[None, :]  10.4 us
    all_to_all x1, waiting for transfers between devices, shards(): lax.all_to_all(query_local, 'head', split_axis=1, concat_axis=0, tiled=True)  9.9 us
  transfers between devices with their start and end apart: 2, of which 2 were waited for; matrix products, arithmetic and copies ran while one was open for 0% of the time, Pallas kernels for 0%

commit v1 on v0

v1 whole, which is shorter than its diff:
```python
import functools
import math

import jax
import jax.numpy as jnp
from jax import lax
from jax.experimental import pallas as pl
from jax.experimental.pallas import tpu as pltpu
from jax.sharding import PartitionSpec as P

QH = 32
KVH = 4
HD = 128
GROUP = QH // KVH
NX, NY, NZ = 4, 4, 8
TOK = 64
ROWS = TOK * GROUP
SPAN = TOK * NY * 2
WIDE = GROUP * HD
TILE = 256
SCALE = math.log2(math.e) / math.sqrt(HD)
LOW = -1e30
MESH = pl.DeviceIdType.MESH


def mod(a, n):
    return lax.rem(a + n, n)


def device(x, y, z, c):
    return (x * 4 + z // 2, y * 4 + lax.rem(z, 2) * 2 + c)


def offset(n):
    d = (n + 1) // 2
    return d * (1 - 2 * lax.rem(n, 2))


def kernel(
    q_hbm, k_hbm, v_hbm, o_hbm,
    kv, qb, ob, q2, m_ref, acc,
    own_sem, qs_sem, qr_sem, ks_sem, kr_sem, os_sem, or_sem,
    piece_recv, sib_send, ring_send, aux_send,
):
    ctx, head = lax.axis_index("ctx"), lax.axis_index("head")
    x, zh = ctx // 4, lax.rem(ctx, 4)
    y, zl, c = head // 4, lax.rem(head, 4) // 2, lax.rem(head, 2)
    z = zh * 2 + zl
    sibling = device(x, y, z, 1 - c)
    z_next, z_prev = device(x, y, mod(z + 1, NZ), c), device(x, y, mod(z - 1, NZ), c)
    y_next, y_prev = device(x, mod(y + 1, NY), z, c), device(x, mod(y - 1, NY), z, c)
    y_far = device(x, mod(y + 2, NY), z, c)
    x_peers = [device(mod(x + i, NX), y, z, c) for i in (1, 2, 3)]

    barrier = pltpu.get_barrier_semaphore()
    peers = [sibling, z_next, z_prev, y_next, y_prev, y_far] + x_peers
    for peer in peers:
        pl.semaphore_signal(barrier, inc=1, device_id=peer, device_id_type=MESH)
    pl.semaphore_wait(barrier, len(peers))

    def part(yy, cc):
        return pl.ds(pl.multiple_of((yy * 2 + cc) * TOK, TOK), TOK)

    def columns(i, width):
        return pl.ds(pl.multiple_of(i * width, width), width)

    mine = part(y, c)

    def kv_copy(i, which, owner):
        peer_x = mod(x + i, NX)
        ref = (k_hbm, v_hbm)[which]
        return pltpu.make_async_remote_copy(
            src_ref=ref.at[:, columns(peer_x, HD)],
            dst_ref=kv.at[z, owner, mine, pl.ds(which * HD, HD)],
            send_sem=ks_sem.at[i, which],
            recv_sem=kr_sem.at[owner, which],
            device_id=x_peers[i - 1],
            device_id_type=MESH,
        )

    def q_copy(i, owner):
        return pltpu.make_async_remote_copy(
            src_ref=q_hbm.at[:, columns(mod(x + i, NX), WIDE)],
            dst_ref=qb.at[owner],
            send_sem=qs_sem.at[i],
            recv_sem=qr_sem.at[owner],
            device_id=x_peers[i - 1],
            device_id_type=MESH,
        )

    def o_copy(i, owner):
        return pltpu.make_async_remote_copy(
            src_ref=ob.at[mod(x + i, NX)],
            dst_ref=o_hbm.at[:, columns(owner, WIDE)],
            send_sem=os_sem.at[i],
            recv_sem=or_sem.at[owner],
            device_id=x_peers[i - 1],
            device_id_type=MESH,
        )

    own_k = pltpu.make_async_copy(
        k_hbm.at[:, columns(x, HD)], kv.at[z, x, mine, pl.ds(0, HD)], own_sem.at[0])
    own_v = pltpu.make_async_copy(
        v_hbm.at[:, columns(x, HD)], kv.at[z, x, mine, pl.ds(HD, HD)], own_sem.at[1])
    own_q = pltpu.make_async_copy(q_hbm.at[:, columns(x, WIDE)], qb.at[x], own_sem.at[2])
    own_o = pltpu.make_async_copy(ob.at[x], o_hbm.at[:, columns(x, WIDE)], own_sem.at[3])

    def piece(zz, yy, cc, peer, send):
        ref = kv.at[zz, :, part(yy, cc), :]
        return pltpu.make_async_remote_copy(
            src_ref=ref, dst_ref=ref, send_sem=send, recv_sem=piece_recv.at[zz, yy, cc],
            device_id=peer, device_id_type=MESH,
        )

    def place(n):
        return mod(z + offset(n), NZ), (n + 1) // 2, lax.rem(n, 2) == 1

    def sends0(n, k, act):
        zz, far, up = place(n)
        def to(peer, sem):
            act(piece(zz, k, 0, peer, sem))
        to_next = (n == 0) | (up & ((far < 3) | ((far == 3) & (k < 2))))
        to_prev = (n == 0) | (~up & ((far < 3) | ((far == 3) & (k >= 2))))
        pl.when(to_next)(lambda: to(z_next, ring_send.at[n, k, 0]))
        pl.when(to_prev)(lambda: to(z_prev, ring_send.at[n, k, 1]))
        to(sibling, sib_send.at[n, k])

    def sends1(n, k, act):
        zz, far, up = place(n)
        yy = mod(y + (0, -1, 1, 2)[k], NY)
        def to(peer, sem):
            act(piece(zz, yy, 1, peer, sem))
        if k == 0:
            even = lax.rem(y, 2) == 0
            to_next = (n == 0) | (up & ((far < 3) | ((far == 3) & even)))
            to_prev = (n == 0) | (~up & ((far < 3) | ((far == 3) & ~even)))
            pl.when(to_next)(lambda: to(z_next, aux_send.at[n, 0]))
            pl.when(to_prev)(lambda: to(z_prev, aux_send.at[n, 1]))
            to(y_next, ring_send.at[n, k, 0])
            to(y_prev, ring_send.at[n, k, 1])
        if k == 1:
            pl.when(lax.rem(zz, 2) == 0)(lambda: to(y_next, ring_send.at[n, k, 0]))
        if k == 2:
            pl.when(lax.rem(zz, 2) == 1)(lambda: to(y_prev, ring_send.at[n, k, 1]))
        to(sibling, sib_send.at[n, k])

    def await_piece(n, yy, cc):
        piece(place(n)[0], yy, cc, sibling, sib_send.at[n, 0]).wait_recv()

    def start(copy):
        copy.start()

    def sent(copy):
        copy.wait_send()

    def serve0(n, k):
        await_piece(n, k, 0)
        sends0(n, k, start)

    def serve1(n, k):
        await_piece(n, mod(y + (0, -1, 1, 2)[k], NY), 1)
        sends1(n, k, start)

    def far_sends(act):
        @pl.when(c == 0)
        def _():
            for i, peer in enumerate((y_next, y_prev, y_far)):
                act(piece(z, y, 0, peer, aux_send.at[i, 0]))

    for i in (1, 2, 3):
        for which in (0, 1):
            kv_copy(i, which, x).start()
    own_k.start()
    own_v.start()
    for i in (1, 2, 3):
        q_copy(i, x).start()
    own_q.start()
    own_k.wait()
    own_v.wait()
    for i in (1, 2, 3):
        for which in (0, 1):
            kv_copy(i, which, mod(x - i, NX)).wait_recv()
    far_sends(start)

    m_ref[...] = jnp.full_like(m_ref, LOW)
    acc[...] = jnp.zeros_like(acc)

    @pl.when(c == 0)
    def _():
        sends0(0, y, start)
        def others(i, _):
            serve0(0, mod(y + i, NY))
            return 0
        lax.fori_loop(1, NY, others, 0)
        lax.fori_loop(0, NY, lambda k, _: (serve0(1, k), 0)[1], 0)

    @pl.when(c == 1)
    def _():
        sends1(0, 0, start)
        serve1(1, 0)
        serve1(0, 1)
        serve1(0, 2)
        serve1(2, 0)
        serve1(1, 1)
        serve1(1, 2)
        serve1(0, 3)

    own_q.wait()
    for i in (1, 2, 3):
        q_copy(i, mod(x - i, NX)).wait_recv()

    def prepare(r, _):
        for g in range(GROUP):
            full = qb[r, :, g * HD:(g + 1) * HD].astype(jnp.float32) * SCALE
            high = full.astype(jnp.bfloat16)
            rows = pl.ds(pl.multiple_of(r * ROWS + g * TOK, TOK), TOK)
            q2[rows, :HD] = high
            q2[rows, HD:] = (full - high.astype(jnp.float32)).astype(jnp.bfloat16)
        return 0

    lax.fori_loop(0, NX, prepare, 0)

    def attend(zz, r, diagonal):
        spans = r + 1 if diagonal else r
        if not spans:
            return
        keys = kv[zz, :spans, :, :HD].reshape(spans * SPAN, HD)
        values = kv[zz, :spans, :, HD:].reshape(spans * SPAN, HD)
        keys = jnp.concatenate([keys, keys], axis=1)
        values = jnp.concatenate([values, jnp.ones_like(values)], axis=1)
        tiles = [pl.ds(r * ROWS + i * TILE, TILE) for i in range(ROWS // TILE)]
        scores = [
            lax.dot_general(
                q2[t, :], keys, (((1,), (1,)), ((), ())), preferred_element_type=jnp.float32)
            for t in tiles
        ]
        old = [m_ref[t, :] for t in tiles]
        sums = [acc[t, :] for t in tiles]
        if diagonal:
            lane = lax.broadcasted_iota(jnp.int32, (TILE, HD), 1)
            row = lax.rem(lax.broadcasted_iota(jnp.int32, (TILE, HD), 0), TOK)
            ahead = lane - row
            span_gap = (zh - zz // 2) * (2 * SPAN) + head * TOK - lax.rem(zz, 2) * 2 * TOK
        done = []
        for score, peak, total in zip(scores, old, sums):
            cols = [score[:, j * HD:(j + 1) * HD] for j in range(spans * SPAN // HD)]
            if diagonal:
                for j in range(SPAN // HD):
                    at = len(cols) - SPAN // HD + j
                    cols[at] = jnp.where(ahead <= span_gap - j * 4 * TOK, cols[at], LOW)
            top = cols
            while len(top) > 1:
                rest = top[len(top) // 2 * 2:]
                top = [jnp.maximum(a, b) for a, b in zip(top[::2], top[1::2])] + rest
            top = jnp.maximum(peak, jnp.max(top[0], axis=1, keepdims=True))
            factor = jnp.exp2(peak - top)
            weights = jnp.concatenate(
                [jnp.exp2(col - top).astype(jnp.bfloat16) for col in cols], axis=1)
            added = jnp.dot(weights, values, preferred_element_type=jnp.float32)
            total = jnp.concatenate([total[:, :HD] * factor, total[:, HD:] * factor], axis=1)
            done.append((total + added, top))
        for t, (total, top) in zip(tiles, done):
            acc[t, :] = total
            m_ref[t, :] = top

    def block(n, _):
        zz = mod(z + offset(n), NZ)
        lax.fori_loop(0, NY, lambda k, _: (await_piece(n, k, 1 - c), 0)[1], 0)
        for slot, r in enumerate((3, 2, 1, 0)):
            ahead = (3, 2, 2, 1)[slot]
            pl.when((c == 0) & (n + 2 < NZ))(lambda: serve0(n + 2, slot))
            pl.when((c == 1) & (n + ahead < NZ))(lambda: serve1(n + ahead, slot))
            inside = zz // 2 <= zh
            pl.when(inside)(lambda: attend(zz, r, True))
            pl.when(~inside)(lambda: attend(zz, r, False))
        return 0

    lax.fori_loop(0, NZ, block, 0)

    def finish(r):
        for g in range(GROUP):
            rows = pl.ds(pl.multiple_of(r * ROWS + g * TOK, TOK), TOK)
            out = acc[rows, :HD] / acc[rows, HD:]
            ob[r, :, g * HD:(g + 1) * HD] = out.astype(jnp.bfloat16)

    for i in (2, 1, 3):
        finish(mod(x + i, NX))
        o_copy(i, x).start()
    finish(x)
    own_o.start()

    for i in (1, 2, 3):
        for which in (0, 1):
            kv_copy(i, which, x).wait_send()
        q_copy(i, x).wait_send()
    far_sends(sent)
    def drain(n, _):
        for k in range(4):
            pl.when(c == 0)(lambda: sends0(n, k, sent))
            pl.when(c == 1)(lambda: sends1(n, k, sent))
        return 0
    lax.fori_loop(0, NZ, drain, 0)
    own_o.wait()
    for i in (1, 2, 3):
        o_copy(i, x).wait_send()
        o_copy(i, mod(x - i, NX)).wait_recv()


def shards(queries, keys, values):
    dma = pltpu.SemaphoreType.DMA
    return pl.pallas_call(
        kernel,
        out_shape=jax.ShapeDtypeStruct(queries.shape, jnp.bfloat16),
        in_specs=[pl.BlockSpec(memory_space=pl.ANY)] * 3,
        out_specs=pl.BlockSpec(memory_space=pl.ANY),
        scratch_shapes=[
            pltpu.VMEM((NZ, NX, SPAN, 2 * HD), jnp.bfloat16),
            pltpu.VMEM((NX, TOK, WIDE), jnp.bfloat16),
            pltpu.VMEM((NX, TOK, WIDE), jnp.bfloat16),
            pltpu.VMEM((NX * ROWS, 2 * HD), jnp.bfloat16),
            pltpu.VMEM((NX * ROWS, HD), jnp.float32),
            pltpu.VMEM((NX * ROWS, 2 * HD), jnp.float32),
            dma((4,)), dma((4,)), dma((4,)), dma((4, 2)), dma((4, 2)), dma((4,)), dma((4,)),
            dma((NZ, NY, 2)), dma((NZ, 4)), dma((NZ, 4, 2)), dma((NZ, 2)),
        ],
        compiler_params=pltpu.CompilerParams(
            collective_id=0, has_side_effects=True, vmem_limit_bytes=56 << 20),
        cost_estimate=pl.CostEstimate(
            flops=9 << 30, bytes_accessed=2 << 20, transcendentals=17 << 20),
    )(queries, keys, values)


def solution(mesh):
    spec = P(("ctx", "head"), None)
    return jax.shard_map(
        shards, mesh=mesh, in_specs=(spec, spec, spec), out_specs=spec, check_vma=False)
```

time: 313 us -> 71.7 us (0.23)
  the two profiles are of different devices: /device:TPU:231 before, /device:TPU:224 now
where the time goes in v1:
time: 71.7 us; the launch traced here: 71.5 us
  Pallas kernels  69.7 us (97%)
  local copies, waits for them, and re-layouts  1.87 us (3%)
    pallas_call x1, Pallas kernels, shards(): pl.pallas_call(kernel, out_shape=jax.ShapeDtypeStruct(queries.shape, jnp....  69.7 us
    unnamed x1, local copies, waits for them, and re-layouts  1.87 us

profile of v1, /device:TPU:224, one launch (start us, length us, event | category | flops | bytes accessed | tf_op | source)
XLA Modules:
  0.0 71.5 jit_solution(6451706442548044300)
XLA Ops:
  0.0 69.7 %shard_map.37 = bf16[64,4096]{1,0:T(8,128)(2,1)} custom-call(bf16[64,4096]{1,0:T(8,128)(2,1)} %q_hbm.1, bf16[64,512]{1,0:T(8,128)(2,1)} %k_hbm.1, bf16[64,512]{1,0:T(8,128)(2,1)} %v_hbm.1), custom_call_target="tpu_custom_call" | custom-call | flops 9663676416 | bytes 2097152 | tf_op jit(solution)/shard_map/pallas_call | solution.py:311
  69.7 1.9 %copy.5 = bf16[64,4096]{1,0:T(8,128)(2,1)} copy(bf16[64,4096]{1,0:T(8,128)(2,1)} %shard_map.37) | data formatting | bytes 1048576

commit v2 on v1

v2 whole, which is shorter than its diff:
```python
import functools
import math

import jax
import jax.numpy as jnp
from jax import lax
from jax.experimental import pallas as pl
from jax.experimental.pallas import tpu as pltpu
from jax.sharding import PartitionSpec as P

QH = 32
KVH = 4
HD = 128
GROUP = QH // KVH
NX, NY, NZ = 4, 4, 8
TOK = 64
ROWS = TOK * GROUP
SPAN = TOK * NY * 2
WIDE = GROUP * HD
TILE = 256
SCALE = math.log2(math.e) / math.sqrt(HD)
LOW = -1e30
HELD = 2
MESH = pl.DeviceIdType.MESH


def mod(a, n):
    return lax.rem(a + n, n)


def device(x, y, z, c):
    return (x * 4 + z // 2, y * 4 + lax.rem(z, 2) * 2 + c)


def offset(n):
    d = (n + 1) // 2
    return d * (1 - 2 * lax.rem(n, 2))


def kernel(
    q_hbm, k_hbm, v_hbm, o_hbm,
    kv, qb, ob, m_ref, acc,
    own_sem, qs_sem, qr_sem, ks_sem, kr_sem, os_sem, or_sem,
    piece_recv, sib_recv, sib_send, ring_send, aux_send,
):
    ctx, head = lax.axis_index("ctx"), lax.axis_index("head")
    x, zh = ctx // 4, lax.rem(ctx, 4)
    y, zl, c = head // 4, lax.rem(head, 4) // 2, lax.rem(head, 2)
    z = zh * 2 + zl
    sibling = device(x, y, z, 1 - c)
    z_next, z_prev = device(x, y, mod(z + 1, NZ), c), device(x, y, mod(z - 1, NZ), c)
    y_next, y_prev = device(x, mod(y + 1, NY), z, c), device(x, mod(y - 1, NY), z, c)
    y_far = device(x, mod(y + 2, NY), z, c)
    x_peers = [device(mod(x + i, NX), y, z, c) for i in (1, 2, 3)]

    barrier = pltpu.get_barrier_semaphore()
    peers = [sibling, z_next, z_prev, y_next, y_prev, y_far] + x_peers
    for peer in peers:
        pl.semaphore_signal(barrier, inc=1, device_id=peer, device_id_type=MESH)
    pl.semaphore_wait(barrier, len(peers))

    def part(yy, cc):
        return pl.ds(pl.multiple_of((cc * NY + yy) * TOK, TOK), TOK)

    def columns(i, width):
        return pl.ds(pl.multiple_of(i * width, width), width)

    mine = part(y, c)

    def kv_copy(i, which, owner):
        peer_x = mod(x + i, NX)
        ref = (k_hbm, v_hbm)[which]
        return pltpu.make_async_remote_copy(
            src_ref=ref.at[:, columns(peer_x, HD)],
            dst_ref=kv.at[z, owner, mine, pl.ds(which * HD, HD)],
            send_sem=ks_sem.at[i, which],
            recv_sem=kr_sem.at[owner, which],
            device_id=x_peers[i - 1],
            device_id_type=MESH,
        )

    def q_copy(i):
        return pltpu.make_async_remote_copy(
            src_ref=q_hbm.at[:, columns(mod(x + i, NX), WIDE)],
            dst_ref=qb.at[x],
            send_sem=qs_sem.at[i],
            recv_sem=qr_sem.at[x],
            device_id=x_peers[i - 1],
            device_id_type=MESH,
        )

    def q_arrival(r):
        return pltpu.make_async_remote_copy(
            src_ref=qb.at[r], dst_ref=qb.at[r], send_sem=qs_sem.at[0], recv_sem=qr_sem.at[r],
            device_id=sibling, device_id_type=MESH,
        )

    def o_copy(r, owner):
        return pltpu.make_async_remote_copy(
            src_ref=ob.at[r],
            dst_ref=o_hbm.at[:, columns(owner, WIDE)],
            send_sem=os_sem.at[r],
            recv_sem=or_sem.at[owner],
            device_id=device(r, y, z, c),
            device_id_type=MESH,
        )

    own_k = pltpu.make_async_copy(
        k_hbm.at[:, columns(x, HD)], kv.at[z, x, mine, pl.ds(0, HD)], own_sem.at[0])
    own_v = pltpu.make_async_copy(
        v_hbm.at[:, columns(x, HD)], kv.at[z, x, mine, pl.ds(HD, HD)], own_sem.at[1])
    own_q = pltpu.make_async_copy(q_hbm.at[:, columns(x, WIDE)], qb.at[x], own_sem.at[2])
    own_o = pltpu.make_async_copy(ob.at[x], o_hbm.at[:, columns(x, WIDE)], own_sem.at[3])

    def piece(zz, yy, cc, peer, send):
        ref = kv.at[zz, :, part(yy, cc), :]
        return pltpu.make_async_remote_copy(
            src_ref=ref, dst_ref=ref, send_sem=send, recv_sem=piece_recv.at[zz, yy, cc],
            device_id=peer, device_id_type=MESH,
        )

    def half(zz, n, cc):
        ref = kv.at[zz, :, pl.ds(pl.multiple_of(cc * NY * TOK, NY * TOK), NY * TOK), :]
        return pltpu.make_async_remote_copy(
            src_ref=ref, dst_ref=ref, send_sem=sib_send.at[n, 0], recv_sem=sib_recv.at[n],
            device_id=sibling, device_id_type=MESH,
        )

    def to_sibling(n, k, cc, act):
        zz = place(n)[0]
        def one():
            act(piece(zz, mod(y + offset(k), NY), cc, sibling, sib_send.at[0, k]))
        pl.when(n == 0)(one)
        pl.when((n > 0) & (k == NY - 1))(lambda: act(half(zz, n, cc)))

    def await_sibling(n):
        def pieces():
            for k in range(NY):
                await_piece(0, k, 1 - c)
        pl.when(n == 0)(pieces)
        pl.when(n > 0)(lambda: half(place(n)[0], n, 1 - c).wait_recv())

    def place(n):
        return mod(z + offset(n), NZ), (n + 1) // 2, lax.rem(n, 2) == 1

    def sends0(n, k, act):
        zz, far, up = place(n)
        def to(peer, sem):
            act(piece(zz, mod(y + offset(k), NY), 0, peer, sem))
        to_sibling(n, k, 0, act)
        to_next = (n == 0) | (up & ((far < 3) | ((far == 3) & (k < 2))))
        to_prev = (n == 0) | (~up & ((far < 3) | ((far == 3) & (k >= 2))))
        pl.when(to_next)(lambda: to(z_next, ring_send.at[n, k, 0]))
        pl.when(to_prev)(lambda: to(z_prev, ring_send.at[n, k, 1]))

    def sends1(n, k, act):
        zz, far, up = place(n)
        def to(peer, sem):
            act(piece(zz, mod(y + offset(k), NY), 1, peer, sem))
        to_sibling(n, k, 1, act)
        if k == 0:
            even = lax.rem(y, 2) == 0
            to_next = (n == 0) | (up & ((far < 3) | ((far == 3) & even)))
            to_prev = (n == 0) | (~up & ((far < 3) | ((far == 3) & ~even)))
            pl.when(to_next)(lambda: to(z_next, ring_send.at[n, 3, 0]))
            pl.when(to_prev)(lambda: to(z_prev, ring_send.at[n, 3, 1]))

    def along_y(n, cc, act):
        for i, peer in enumerate((y_next, y_prev, y_far)):
            act(piece(place(n)[0], y, cc, peer, aux_send.at[n, i]))

    def await_piece(n, k, cc):
        yy = mod(y + offset(k), NY)
        piece(place(n)[0], yy, cc, sibling, sib_send.at[n, k]).wait_recv()

    def start(copy):
        copy.start()

    def sent(copy):
        copy.wait_send()

    def serve0(n, k):
        await_piece(n, k, 0)
        sends0(n, k, start)

    def relay1(n, k):
        await_piece(n, k, 1)
        to_sibling(n, k, 1, start)

    def serve1(n, k):
        await_piece(n, k, 1)
        sends1(n, k, start)
        if k == 0:
            if n >= HELD:
                along_y(n - HELD, 1, sent)
            along_y(n, 1, start)

    def pair0(d, k):
        serve0(2 * d - 1, k)
        serve0(2 * d, k)

    for i in (1, 2, 3):
        for which in (0, 1):
            kv_copy(i, which, x).start()
    own_k.start()
    own_v.start()
    for i in (1, 3):
        q_copy(i).start()
    own_q.start()
    own_k.wait()
    own_v.wait()
    for i in (1, 2, 3):
        for which in (0, 1):
            kv_copy(i, which, mod(x - i, NX)).wait_recv()

    @pl.when(c == 0)
    def _():
        sends0(0, 0, start)
        along_y(0, 0, start)

    @pl.when(c == 1)
    def _():
        sends1(0, 0, start)
        along_y(0, 1, start)

    q_copy(2).start()
    m_ref[...] = jnp.full_like(m_ref, LOW)
    acc[...] = jnp.zeros_like(acc)

    @pl.when(c == 0)
    def _():
        lax.fori_loop(1, NY, lambda k, _: (serve0(0, k), 0)[1], 0)

    @pl.when(c == 1)
    def _():
        lax.fori_loop(1, NY, lambda k, _: (relay1(0, k), 0)[1], 0)
        serve1(1, 0)
        serve1(2, 0)

    def attend(zz, r, diagonal):
        spans = r + 1 if diagonal else r
        if not spans:
            return
        keys = kv[zz, :spans, :, :HD].reshape(spans * SPAN, HD)
        values = kv[zz, :spans, :, HD:].reshape(spans * SPAN, HD)
        values = jnp.concatenate([values, jnp.ones_like(values)], axis=1)
        tiles = [pl.ds(r * ROWS + i * TILE, TILE) for i in range(ROWS // TILE)]
        scores = []
        for i in range(len(tiles)):
            heads = range(i * TILE // TOK, (i + 1) * TILE // TOK)
            query = jnp.concatenate([qb[r, :, g * HD:(g + 1) * HD] for g in heads], axis=0)
            scores.append(lax.dot_general(
                query, keys, (((1,), (1,)), ((), ())), preferred_element_type=jnp.float32))
        old = [m_ref[t, :] for t in tiles]
        sums = [acc[t, :] for t in tiles]
        if diagonal:
            lane = lax.broadcasted_iota(jnp.int32, (TILE, HD), 1)
            row = lax.rem(lax.broadcasted_iota(jnp.int32, (TILE, HD), 0), TOK)
            ahead = lane // TOK * (4 * TOK) + lax.rem(lane, TOK) - row
            span_gap = (zh - zz // 2) * (2 * SPAN) + head * TOK - lax.rem(zz, 2) * 2 * TOK
        done = []
        for score, peak, total in zip(scores, old, sums):
            cols = [score[:, j * HD:(j + 1) * HD] for j in range(spans * SPAN // HD)]
            if diagonal:
                for j in range(SPAN // HD):
                    at = len(cols) - SPAN // HD + j
                    cols[at] = jnp.where(
                        ahead <= span_gap - (j % 2 * 8 + j // 2) * TOK, cols[at], LOW)
            top = cols
            while len(top) > 1:
                rest = top[len(top) // 2 * 2:]
                top = [jnp.maximum(a, b) for a, b in zip(top[::2], top[1::2])] + rest
            top = jnp.maximum(peak, jnp.max(top[0], axis=1, keepdims=True))
            factor = jnp.exp2((peak - top) * SCALE)
            weights = jnp.concatenate(
                [jnp.exp2((col - top) * SCALE).astype(jnp.bfloat16) for col in cols], axis=1)
            added = jnp.dot(weights, values, preferred_element_type=jnp.float32)
            total = jnp.concatenate([total[:, :HD] * factor, total[:, HD:] * factor], axis=1)
            done.append((total + added, top))
        for t, (total, top) in zip(tiles, done):
            acc[t, :] = total
            m_ref[t, :] = top

    def finish(r):
        for g in range(GROUP):
            rows = pl.ds(pl.multiple_of(r * ROWS + g * TOK, TOK), TOK)
            out = acc[rows, :HD] / acc[rows, HD:]
            ob[r, :, g * HD:(g + 1) * HD] = out.astype(jnp.bfloat16)

    def work(w, _):
        last = w >= 4 * (NZ - 2)
        slot = jnp.where(last, (w - 4 * (NZ - 2)) // 2, lax.rem(w, 4))
        n = jnp.where(last, NZ - 2 + lax.rem(w, 2), w // 4)
        near = slot + jnp.where(slot == 2, 1, 0) - jnp.where(slot == 3, 1, 0)
        turn = lax.rem(x + jnp.where(last, slot + 1, near), NX)
        r = jnp.where(last | (n == 0), turn, 3 - slot)
        zz = mod(z + offset(n), NZ)

        @pl.when(jnp.where(last, w < 4 * (NZ - 2) + 2, slot == 0))
        def _():
            await_sibling(n)

        @pl.when((c == 0) & (n < 6))
        def _():
            @pl.when((n == 0) & (slot > 0))
            def _():
                pair0(1, slot - 1)
                pl.when(slot == 3)(lambda: pair0(1, 3))

            @pl.when((n > 0) & (n < 5))
            def _():
                far = (n - 1) // 2 + 2
                serve0(2 * far - 1 + lax.rem(slot, 2), 2 * lax.rem(n + 1, 2) + slot // 2)

            @pl.when((n == 5) & (slot > 1))
            def _():
                serve0(7, slot - 2)
                serve0(7, slot)

        @pl.when((c == 1) & (n < 6))
        def _():
            for at, at_slot, m in ((0, 1, 3), (0, 2, 4), (1, 0, 5), (1, 1, 6), (2, 0, 7)):
                pl.when((n == at) & (slot == at_slot))(lambda: serve1(m, 0))
            pl.when(slot > 0)(lambda: relay1(n + 1, slot))

            @pl.when((n == 5) & (slot == 3))
            def _():
                lax.fori_loop(1, NY, lambda k, _: (relay1(7, k), 0)[1], 0)

        @pl.when(n == 0)
        def _():
            pl.when(r == x)(own_q.wait)
            pl.when(r != x)(lambda: q_arrival(r).wait_recv())

        for quarter in range(NX):
            inside = zz // 2 <= zh
            pl.when((r == quarter) & inside)(lambda: attend(zz, quarter, True))
            pl.when((r == quarter) & ~inside)(lambda: attend(zz, quarter, False))

        @pl.when(last & (lax.rem(w, 2) == 1))
        def _():
            finish(r)
            pl.when(r != x)(lambda: o_copy(r, x).start())
            pl.when(r == x)(own_o.start)
        return 0

    lax.fori_loop(0, 4 * NZ, work, 0)

    for i in (1, 2, 3):
        for which in (0, 1):
            kv_copy(i, which, x).wait_send()
        q_copy(i).wait_send()
    pl.when(c == 0)(lambda: along_y(0, 0, sent))

    @pl.when(c == 1)
    def _():
        for n in range(NZ - HELD, NZ):
            along_y(n, 1, sent)

    def drain(n, _):
        for k in range(4):
            pl.when(c == 0)(lambda: sends0(n, k, sent))
            pl.when(c == 1)(lambda: sends1(n, k, sent))
        return 0

    lax.fori_loop(0, NZ, drain, 0)
    own_o.wait()
    for r in range(NX):
        pl.when(r != x)(lambda: o_copy(r, x).wait_send())
        pl.when(r != x)(lambda: o_copy(r, r).wait_recv())


def shards(queries, keys, values):
    dma = pltpu.SemaphoreType.DMA
    return pl.pallas_call(
        kernel,
        out_shape=jax.ShapeDtypeStruct(queries.shape, jnp.bfloat16),
        in_specs=[pl.BlockSpec(memory_space=pl.ANY)] * 3,
        out_specs=pl.BlockSpec(memory_space=pl.ANY),
        scratch_shapes=[
            pltpu.VMEM((NZ, NX, SPAN, 2 * HD), jnp.bfloat16),
            pltpu.VMEM((NX, TOK, WIDE), jnp.bfloat16),
            pltpu.VMEM((NX, TOK, WIDE), jnp.bfloat16),
            pltpu.VMEM((NX * ROWS, HD), jnp.float32),
            pltpu.VMEM((NX * ROWS, 2 * HD), jnp.float32),
            dma((4,)), dma((4,)), dma((4,)), dma((4, 2)), dma((4, 2)), dma((4,)), dma((4,)),
            dma((NZ, NY, 2)), dma((NZ,)), dma((NZ, 4)), dma((NZ, 4, 2)), dma((NZ, 3)),
        ],
        compiler_params=pltpu.CompilerParams(
            collective_id=0, has_side_effects=True, vmem_limit_bytes=56 << 20),
        cost_estimate=pl.CostEstimate(
            flops=9 << 30, bytes_accessed=2 << 20, transcendentals=17 << 20),
    )(queries, keys, values)


def solution(mesh):
    spec = P(("ctx", "head"), None)
    return jax.shard_map(
        shards, mesh=mesh, in_specs=(spec, spec, spec), out_specs=spec, check_vma=False)
```

time: 71.7 us -> 69 us (0.962)
  the two profiles are of different devices: /device:TPU:224 before, /device:TPU:231 now
where the time goes in v2:
time: 69 us; the launch traced here: 67.9 us
  Pallas kernels  66 us (96%)
  local copies, waits for them, and re-layouts  1.87 us (3%)
    pallas_call x1, Pallas kernels, shards(): pl.pallas_call(kernel, out_shape=jax.ShapeDtypeStruct(queries.shape, jnp....  66 us
    unnamed x1, local copies, waits for them, and re-layouts  1.87 us

profile of v2, /device:TPU:231, one launch (start us, length us, event | category | flops | bytes accessed | tf_op | source)
XLA Modules:
  0.0 67.9 jit_solution(5424263992994032712)
XLA Ops:
  0.0 66.0 %shard_map.37 = bf16[64,4096]{1,0:T(8,128)(2,1)} custom-call(bf16[64,4096]{1,0:T(8,128)(2,1)} %q_hbm.1, bf16[64,512]{1,0:T(8,128)(2,1)} %k_hbm.1, bf16[64,512]{1,0:T(8,128)(2,1)} %v_hbm.1), custom_call_target="tpu_custom_call" | custom-call | flops 9663676416 | bytes 2097152 | tf_op jit(solution)/shard_map/pallas_call | solution.py:375
  66.0 1.9 %copy.5 = bf16[64,4096]{1,0:T(8,128)(2,1)} copy(bf16[64,4096]{1,0:T(8,128)(2,1)} %shard_map.37) | data formatting | bytes 1048576

commit v3 on v2

--- a/solution.py
+++ b/solution.py
@@ -319,7 +319,7 @@
 
         @pl.when((c == 1) & (n < 6))
         def _():
-            for at, at_slot, m in ((0, 1, 3), (0, 2, 4), (1, 0, 5), (1, 1, 6), (2, 0, 7)):
+            for at, at_slot, m in ((0, 2, 3), (0, 3, 4), (1, 1, 5), (1, 2, 6), (2, 1, 7)):
                 pl.when((n == at) & (slot == at_slot))(lambda: serve1(m, 0))
             pl.when(slot > 0)(lambda: relay1(n + 1, slot))
 

time: 69 us -> 68.2 us (0.988)
  no operation moved by 1% of the time
where the time goes in v3:
time: 68.2 us; the launch traced here: 67.8 us
  Pallas kernels  65.9 us (97%)
  local copies, waits for them, and re-layouts  1.87 us (3%)
    pallas_call x1, Pallas kernels, shards(): pl.pallas_call(kernel, out_shape=jax.ShapeDtypeStruct(queries.shape, jnp....  65.9 us
    unnamed x1, local copies, waits for them, and re-layouts  1.87 us

profile of v3, /device:TPU:231, one launch (start us, length us, event | category | flops | bytes accessed | tf_op | source)
XLA Modules:
  0.0 67.8 jit_solution(14825001320135216128)
XLA Ops:
  0.0 65.9 %shard_map.37 = bf16[64,4096]{1,0:T(8,128)(2,1)} custom-call(bf16[64,4096]{1,0:T(8,128)(2,1)} %q_hbm.1, bf16[64,512]{1,0:T(8,128)(2,1)} %k_hbm.1, bf16[64,512]{1,0:T(8,128)(2,1)} %v_hbm.1), custom_call_target="tpu_custom_call" | custom-call | flops 9663676416 | bytes 2097152 | tf_op jit(solution)/shard_map/pallas_call | solution.py:375
  65.9 1.9 %copy.5 = bf16[64,4096]{1,0:T(8,128)(2,1)} copy(bf16[64,4096]{1,0:T(8,128)(2,1)} %shard_map.37) | data formatting | bytes 1048576
